TPU v7x, 256 devices: a whole 4x4x8 slice. The times are simulated.
256 devices in a mesh: row: 16 (over x_lo, y, core), col: 16 (over x_hi, z).
Axes of the slice: x: 4 (x_hi: 2, x_lo: 2; x = x_hi * 2 + x_lo), y: 4, z: 8, core: 2. Of those that a mesh axis runs over, the one named last changes fastest.
Arguments:
- matrix: float32 [16384, 24576], P('col', 'row')
- inverse: float32 [256, 256], replicated, as said below
- pivots: int32 [256], replicated, may hold values from 256 to 16383, as said below
Outputs:
- factored: float32 [16384, 24576], P('col', 'row')
Inputs may be any that keep to these rules, and one draw needn't show every extreme that they name: The 256 pivots are distinct and none lies among the top 256 rows. `inverse`: unit lower triangular.
All inputs are finite; a program needn't handle non-finite values.
Results may differ from a plain program's by a relative error of at most 0.0033.
Values may be sent and summed in bfloat16 or wider, within the bound.
A program may use at most 128 MiB of HBM per device.

v0:
```python
import jax
import jax.numpy as jnp
from jax import lax
from jax.sharding import PartitionSpec as P


def from_root(array, axis, root):
    mine = lax.axis_index(axis) == root
    return lax.psum(jnp.where(mine, array, jnp.zeros_like(array)), axis)


def solve_rows(inverse, block):
    return jnp.dot(
        inverse, block, precision=lax.Precision.HIGHEST, preferred_element_type=jnp.float32
    )


def per_device(matrix, inverse, pivots):
    rows_dev, cols_dev = matrix.shape
    block_width = inverse.shape[0]
    grid_col = lax.axis_index("col")
    grid_row = lax.axis_index("row")
    row_start = grid_col * rows_dev
    col_start = grid_row * cols_dev
    local_rows = pivots - row_start
    owned_here = (local_rows >= 0) & (local_rows < rows_dev)
    picked = jnp.take(matrix, jnp.clip(local_rows, 0, rows_dev - 1), axis=0)
    picked = jnp.where(owned_here[:, None], picked, 0.0)
    panel_rows = from_root(matrix[:, :block_width].astype(jnp.bfloat16), "row", 0)
    pivot_block = lax.psum(picked, "col")
    top_block = from_root(matrix[:block_width].astype(jnp.bfloat16), "col", 0).astype(jnp.float32)
    upper_rows = solve_rows(inverse, pivot_block)
    target = jnp.where(owned_here, local_rows, rows_dev)
    swapped = matrix.at[target].set(top_block, mode="drop")
    product = jnp.dot(
        panel_rows, upper_rows.astype(jnp.bfloat16), preferred_element_type=jnp.float32
    )
    updated = swapped - product
    updated = updated.at[:block_width].set(
        jnp.where(grid_col == 0, upper_rows, updated[:block_width])
    )
    column_ids = col_start + jnp.arange(cols_dev)
    return jnp.where((column_ids < block_width)[None, :], matrix, updated)


def solution(mesh):
    return jax.shard_map(
        per_device,
        mesh=mesh,
        in_specs=(P("col", "row"), P(), P()),
        out_specs=P("col", "row"),
        check_vma=False,
    )
```

profile of v0, /device:TPU:49, one launch (start us, length us, event | category | flops | bytes accessed | tf_op | source)
XLA Modules:
  0.0 487.8 jit_solution(11441301336407350465)
XLA Ops:
  6.5 0.0 copy-start
  6.5 0.0 all-reduce.4.cloned.1.call-start
  6.5 6.0 %copy.17 = f32[1024,1536]{1,0:T(8,128)} copy(f32[1024,1536]{1,0:T(8,128)} %param.5) | data formatting | bytes 12582912
  12.5 6.6 %copy.8 = f32[1024,1536]{0,1:T(8,128)} copy(f32[1024,1536]{1,0:T(8,128)} %copy.17) | data formatting | bytes 12582912 | tf_op args[0]
  19.1 3.3 convert.4
  22.4 0.0 copy-start.1
  22.4 1.0 slice_select_fusion.1
  23.4 0.0 all-reduce.4.cloned.1.call-update
  23.4 0.0 all-reduce.8.cloned.1.call-start
  23.5 0.0 copy-done.1
  23.5 5.9 %gather_fusion = f32[256,1536]{1,0:T(8,128)} fusion(f32[1024,1536]{1,0:T(8,128)} %copy.17, s32[1024]{0:T(1024)S(1)} %pad_clamp_fusion), kind=kCustom, calls=%fused_computation | custom fusion | bytes 3146752 | tf_op jit(solution)/shard_map/jit(_take)/gather | solution.py:27
  29.4 2.8 select_select_fusion
  32.2 0.0 all-reduce.8.cloned.1.call-update
  32.2 0.0 all-reduce.6.cloned.1.call-start
  32.2 0.8 slice_select_fusion.2
  33.1 0.0 all-reduce.6.cloned.1.call-update
  33.1 138.7 %all-reduce.4.cloned.1.call-done = bf16[256,1536]{0,1:T(8,128)(2,1)} async-done(((bf16[256,1536]{0,1:T(8,128)(2,1)}), bf16[256,1536]{0,1:T(8,128)(2,1)}) %all-reduce.4.cloned.1.call-update) | async-done | bytes 786448 | tf_op jit(solution)/shard_map/psum | solution.py:9
  171.8 1.4 copy.5
  173.2 7.0 %scatter_fusion = f32[1024,1536]{1,0:T(8,128)} fusion(f32[1024,1536]{1,0:T(8,128)} %copy.17, s32[256]{0:T(256)S(1)} %compare_select_fusion.1, f32[256,1536]{1,0:T(8,128)S(1)} %copy.5), kind=kCustom, calls=%fused_computation.1 | custom fusion | bytes 4719616 | tf_op jit(solution)/shard_map/scatter | solution.py:34
  180.3 6.5 %copy.6 = f32[1024,1536]{0,1:T(8,128)} copy(f32[1024,1536]{1,0:T(8,128)} %scatter_fusion) | data formatting | bytes 12582912 | tf_op jit(solution)/shard_map/scatter | solution.py:34
  186.8 146.1 %all-reduce.8.cloned.1.call-done = f32[256,1536]{1,0:T(8,128)} async-done(((f32[256,1536]{1,0:T(8,128)}), f32[256,1536]{1,0:T(8,128)}) %all-reduce.8.cloned.1.call-update) | async-done | bytes 1572880 | tf_op jit(solution)/shard_map/psum | solution.py:30
  332.9 0.0 copy-done
  332.9 4.0 convolution_bitcast_fusion
  336.9 128.3 %all-reduce.6.cloned.1.call-done = bf16[1024,256]{0,1:T(8,128)(2,1)} async-done(((bf16[1024,256]{0,1:T(8,128)(2,1)}), bf16[1024,256]{0,1:T(8,128)(2,1)}) %all-reduce.6.cloned.1.call-update) | async-done | bytes 524304 | tf_op jit(solution)/shard_map/psum | solution.py:9
  465.3 4.0 convolution_subtract_fusion
  469.2 0.4 fusion
  469.6 5.1 %broadcast_select_fusion = f32[1024,1536]{0,1:T(8,128)} fusion(f32[1024,1536]{0,1:T(8,128)} %copy.8, f32[1024,1536]{0,1:T(8,128)S(1)} %fusion, pred[1536]{0:T(1024)(128)(4,1)S(1)} %add_compare_fusion), kind=kLoop, calls=%fused_computation.3 | loop fusion | flops 1572864 | bytes 18875904 | tf_op jit(solution)/shard_map/jit(_where)/select_n | solution.py:43
  474.7 6.6 %copy.9 = f32[1024,1536]{1,0:T(8,128)} copy(f32[1024,1536]{0,1:T(8,128)} %broadcast_select_fusion) | data formatting | bytes 12582912 | tf_op jit(solution)/shard_map/jit(_where)/select_n | solution.py:43
  (4 shorter events, 0.0 us)
Async XLA Ops:
  6.5 326.4 %copy-start = (f32[256,256]{1,0:T(8,128)S(1)}, f32[256,256]{1,0:T(8,128)}, u32[]{:S(2)}) copy-start(f32[256,256]{1,0:T(8,128)} %param.6) | copy-start | bytes 786436
  6.5 165.3 %all-reduce.4.cloned.1.call-start = ((), (), s32[]{:S(2)}) async-start(), calls=%async_computation | async-start | bytes 1572864 | tf_op jit(solution)/shard_map/psum | solution.py:9
  22.4 1.1 copy-start.1
  23.4 309.5 %all-reduce.8.cloned.1.call-start = ((), (), s32[]{:S(2)}) async-start(), calls=%async_computation.2 | async-start | bytes 3145728 | tf_op jit(solution)/shard_map/psum | solution.py:30
  32.2 433.1 %all-reduce.6.cloned.1.call-start = ((), (), s32[]{:S(2)}) async-start(), calls=%async_computation.1 | async-start | bytes 1048576 | tf_op jit(solution)/shard_map/psum | solution.py:9
Sparse Core Ops, SparseCore 0:
  23.5 148.2 all-reduce.3
  174.6 158.2 all-reduce.7
  335.5 129.6 all-reduce.5
where the time goes:
time: 491 us; the launch traced here: 488 us
  waiting for transfers between devices  413 us (84%)
  local copies, waits for them, and re-layouts  40 us (8%)
  other arithmetic  13.4 us (3%)
  between operations  13.2 us (3%)
  matrix products  7.98 us (2%)
    psum x2, waiting for transfers between devices, from_root(): return lax.psum(jnp.where(mine, array, jnp.zeros_like(array)), axis)  267 us
    psum x1, waiting for transfers between devices, per_device(): pivot_block = lax.psum(picked, 'col')  146 us
    scatter x2, local copies, waits for them, and re-layouts, per_device(): swapped = matrix.at[target].set(top_block, mode='drop')  13.6 us
    unnamed x6, local copies, waits for them, and re-layouts  12.6 us
  transfers between devices with their start and end apart: 3, of which 3 were waited for; matrix products, arithmetic and copies ran while one was open for 6% of the time, Pallas kernels for 0%

commit v1 on v0

v1 whole, which is shorter than its diff:
```python
import functools

import jax
import jax.numpy as jnp
from jax import lax
from jax.experimental import pallas as pl
from jax.experimental.pallas import tpu as pltpu
from jax.sharding import PartitionSpec as P

MESH = pl.DeviceIdType.MESH
NB = 256
CAP = 32
LANES = 128
Z = 8
COLS = 16
CHUNKS = 4
RING = 6


def from_root(array, axis, root):
    mine = lax.axis_index(axis) == root
    return lax.psum(jnp.where(mine, array, jnp.zeros_like(array)), axis)


def any_pivots(matrix, inverse, pivots):
    rows_dev, cols_dev = matrix.shape
    block_width = inverse.shape[0]
    grid_col = lax.axis_index("col")
    grid_row = lax.axis_index("row")
    local_rows = pivots - grid_col * rows_dev
    owned_here = (local_rows >= 0) & (local_rows < rows_dev)
    picked = jnp.take(matrix, jnp.clip(local_rows, 0, rows_dev - 1), axis=0)
    picked = jnp.where(owned_here[:, None], picked, 0.0)
    panel_rows = from_root(matrix[:, :block_width].astype(jnp.bfloat16), "row", 0)
    pivot_block = lax.psum(picked, "col")
    top_block = from_root(matrix[:block_width].astype(jnp.bfloat16), "col", 0).astype(jnp.float32)
    upper_rows = jnp.dot(
        inverse, pivot_block, precision=lax.Precision.HIGHEST, preferred_element_type=jnp.float32
    )
    target = jnp.where(owned_here, local_rows, rows_dev)
    swapped = matrix.at[target].set(top_block, mode="drop")
    product = jnp.dot(
        panel_rows, upper_rows.astype(jnp.bfloat16), preferred_element_type=jnp.float32
    )
    updated = swapped - product
    updated = updated.at[:block_width].set(
        jnp.where(grid_col == 0, upper_rows, updated[:block_width])
    )
    column_ids = grid_row * cols_dev + jnp.arange(cols_dev)
    return jnp.where((column_ids < block_width)[None, :], matrix, updated)


def update_kernel(
    mat_hbm, inv_ref, piv_ref, out_ref,
    picked, gathered, panel, upper, tops, top, perm, hits, idx_v, idx_s,
    load_sem, idx_sem, own_sem, sp_send, sp_recv, pan_send, pan_recv, top_send, top_recv,
    z_send, x_send, up_recv,
):
    rows, cols = out_ref.shape
    tiles = cols // LANES
    part = rows // CHUNKS
    r = lax.axis_index("row")
    c = lax.axis_index("col")
    xlo, y, core = r // 8, (r // 2) % 4, r % 2
    xhi, z = c // Z, c % Z

    def row_dev(xlo_, y_, core_):
        return ((xlo_ * 4 + y_) * 2 + core_, c)

    def col_dev(c_):
        return (r, c_)

    def owner_of(t):
        q = t % RING
        return (t // RING) * Z + (q + 1 + (q >= 3).astype(jnp.int32) + 2 * core) % Z

    zq = (z - 2 * core + Z) % Z
    is_owner = (zq != 0) & (zq != 4)
    my_tile = xhi * RING + jnp.maximum(zq - 1 - (zq > 4).astype(jnp.int32), 0)

    barrier = pltpu.get_barrier_semaphore()
    for k in range(1, COLS):
        pl.semaphore_signal(barrier, inc=1, device_id=col_dev((c + k) % COLS), device_id_type=MESH)
    for dev in (
        row_dev(xlo, y, 1 - core), row_dev(xlo, (y + 1) % 4, core),
        row_dev(xlo, (y + 3) % 4, core), row_dev(1 - xlo, y, core),
    ):
        pl.semaphore_signal(barrier, inc=1, device_id=dev, device_id_type=MESH)

    loads = [
        pltpu.make_async_copy(
            mat_hbm.at[pl.ds(k * part, part)], out_ref.at[pl.ds(k * part, part)], load_sem.at[k]
        )
        for k in range(CHUNKS)
    ]
    for load in loads:
        load.start()

    i_id = lax.broadcasted_iota(jnp.int32, (NB, NB), 0)
    j_id = lax.broadcasted_iota(jnp.int32, (NB, NB), 1)
    piv_row = jnp.broadcast_to(piv_ref[...], (NB, NB))
    piv_col = piv_row.T
    own_row, own_col = piv_row // rows, piv_col // rows
    rank = jnp.sum(((own_row == own_col) & (i_id < j_id)).astype(jnp.int32), axis=0, keepdims=True)
    slot_row = jnp.broadcast_to(own_row[:1] * CAP + rank, (NB, NB))
    slot_col = slot_row.T
    lane = j_id[:, :LANES]
    match = (slot_col[:, :LANES] == c * CAP + lane) & (lane < CAP)
    idx = jnp.sum(
        jnp.where(match, piv_col[:, :LANES] - c * rows + 1, 0), axis=0, keepdims=True
    ) - 1
    idx_v[...] = jnp.maximum(idx, 0)
    idx_copy = pltpu.make_async_copy(idx_v, idx_s, idx_sem)
    idx_copy.start()
    r_id = lax.broadcasted_iota(jnp.int32, (rows, LANES), 0)
    hits[...] = (r_id == jnp.broadcast_to(idx, (rows, LANES))).astype(jnp.float32).astype(jnp.bfloat16)
    top[CAP:, :] = jnp.zeros((LANES - CAP, cols), jnp.bfloat16)
    idx_copy.wait()
    for load in loads:
        load.wait()

    for k in range(CAP):
        row = out_ref[pl.ds(idx_s[0, k], 1), :]
        for t in range(tiles):
            picked[t, k : k + 1, :] = row[:, t * LANES : (t + 1) * LANES]

    pl.semaphore_wait(barrier, COLS - 1 + 4)

    def pick_copy(t):
        return pltpu.make_async_remote_copy(
            src_ref=picked.at[t], dst_ref=gathered.at[c], send_sem=sp_send.at[t],
            recv_sem=sp_recv.at[c], device_id=col_dev(owner_of(t)), device_id_type=MESH,
        )

    def for_tiles(body):
        lax.fori_loop(0, tiles, lambda t, _: (body(t), 0)[1], 0)

    @for_tiles
    def _(t):
        @pl.when(owner_of(t) != c)
        def _():
            pick_copy(t).start()

    def pan_copy(k, child, dev):
        return pltpu.make_async_remote_copy(
            src_ref=panel.at[k], dst_ref=panel.at[k], send_sem=pan_send.at[k, child],
            recv_sem=pan_recv.at[k], device_id=dev, device_id_type=MESH,
        )

    def pan_children(k):
        return [
            ((core == 0) & (y == 0), row_dev(xlo, 1, 0)),
            ((core == 0) & (y == 0), row_dev(xlo, 3, 0)),
            ((core == 0) & (y == 0) & (xlo == 0), row_dev(1, 0, 0)),
            ((core == 0) & (y == (1 if k < CHUNKS // 2 else 3)), row_dev(xlo, 2, 0)),
            (core == 0, row_dev(xlo, y, 1)),
        ]

    def pan_forward(k):
        for child, (cond, dev) in enumerate(pan_children(k)):
            @pl.when(cond)
            def _():
                pan_copy(k, child, dev).start()

    def pan_wait(k):
        pan_copy(k, 0, row_dev(xlo, y, 1 - core)).wait_recv()

    @pl.when(r == 0)
    def _():
        for k in range(CHUNKS):
            panel[k] = out_ref[k * part : (k + 1) * part, :NB].astype(jnp.bfloat16)
            pan_forward(k)

    def top_copy(dst):
        return pltpu.make_async_remote_copy(
            src_ref=tops.at[dst], dst_ref=top.at[pl.ds(0, CAP)], send_sem=top_send.at[dst],
            recv_sem=top_recv, device_id=col_dev(dst), device_id_type=MESH,
        )

    @pl.when(c == 0)
    def _():
        s_id = lax.broadcasted_iota(jnp.int32, (NB, NB), 0)
        block = out_ref[:NB, :].astype(jnp.bfloat16)
        half = NB // CAP
        for h in range(COLS * CAP // NB):
            pick = (slot_row == s_id + h * NB).astype(jnp.float32).astype(jnp.bfloat16)
            sent = jnp.dot(pick, block, preferred_element_type=jnp.float32).astype(jnp.bfloat16)
            tops[h * half : (h + 1) * half] = sent.reshape(half, CAP, cols)
            for dst in range(max(1, h * half), (h + 1) * half):
                top_copy(dst).start()
        pltpu.make_async_copy(tops.at[0], top.at[pl.ds(0, CAP)], own_sem).start()

    for h in range(COLS * CAP // NB):
        place = (slot_col == j_id + h * NB).astype(jnp.float32)
        perm[:, h * NB : (h + 1) * NB] = jnp.dot(
            inv_ref[...], place, precision=lax.Precision.HIGHEST, preferred_element_type=jnp.float32
        )

    depth_one = (core == 0) & (((xlo == 0) & ((y == 1) | (y == 3))) | ((xlo == 1) & (y == 0)))

    @pl.when(depth_one)
    def _():
        for k in range(CHUNKS):
            pan_wait(k)
            pan_forward(k)

    def z_copy(k):
        return pltpu.make_async_remote_copy(
            src_ref=upper.at[my_tile], dst_ref=upper.at[my_tile], send_sem=z_send.at[k],
            recv_sem=up_recv.at[my_tile], device_id=col_dev(xhi * Z + (z + k) % Z), device_id_type=MESH,
        )

    def x_copy(t):
        return pltpu.make_async_remote_copy(
            src_ref=upper.at[t], dst_ref=upper.at[t], send_sem=x_send.at[t],
            recv_sem=up_recv.at[t], device_id=col_dev((1 - xhi) * Z + z), device_id_type=MESH,
        )

    @pl.when(is_owner)
    def _():
        gathered[c] = picked[my_tile]
        for k in range(1, COLS):
            src = (c + k) % COLS
            pltpu.make_async_remote_copy(
                src_ref=picked.at[0], dst_ref=gathered.at[src], send_sem=sp_send.at[0],
                recv_sem=sp_recv.at[src], device_id=col_dev(src), device_id_type=MESH,
            ).wait_recv()
        solved = jnp.dot(
            perm[...], gathered[...].reshape(COLS * CAP, LANES),
            precision=lax.Precision.HIGHEST, preferred_element_type=jnp.float32,
        )
        upper[my_tile] = solved.astype(jnp.bfloat16)
        for k in (4, 3, 5, 2, 6, 1, 7):
            z_copy(k).start()
        x_copy(my_tile).start()

    @pl.when(jnp.logical_not(depth_one) & (r != 0))
    def _():
        for k in range(CHUNKS):
            pan_wait(k)
            pan_forward(k)

    first = xhi * RING
    for q in range(RING):
        @pl.when((first + q != my_tile) | jnp.logical_not(is_owner))
        def _():
            x_copy(first + q).wait_recv()
            x_copy(first + q).start()

    @pl.when(c == 0)
    def _():
        pltpu.make_async_copy(tops.at[0], top.at[pl.ds(0, CAP)], own_sem).wait()

    @pl.when(c != 0)
    def _():
        top_copy(c).wait_recv()

    def trailing(t):
        return (r != 0) | (t >= NB // LANES)

    def columns(t):
        return pl.ds(pl.multiple_of(t * LANES, LANES), LANES)

    taken = jnp.sum(hits[...].astype(jnp.float32), axis=1, keepdims=True) > 0.5

    @for_tiles
    def _(t):
        @pl.when(trailing(t))
        def _():
            moved = jnp.dot(hits[...], top[:, columns(t)], preferred_element_type=jnp.float32)
            out_ref[:, columns(t)] = jnp.where(taken, moved, out_ref[:, columns(t)])

    def apply(t):
        @pl.when(trailing(t))
        def _():
            for k in range(CHUNKS):
                rows_k = pl.ds(k * part, part)
                out_ref[rows_k, columns(t)] = out_ref[rows_k, columns(t)] - jnp.dot(
                    panel[k], upper[t], preferred_element_type=jnp.float32
                )

            @pl.when(c == 0)
            def _():
                out_ref[:NB, columns(t)] = upper[t].astype(jnp.float32)

    def loop(body):
        lax.fori_loop(0, RING, lambda q, _: (body(q), 0)[1], 0)

    @loop
    def _(q):
        apply(first + q)

    @loop
    def _(q):
        t = (1 - xhi) * RING + q
        x_copy(t).wait_recv()
        apply(t)

    @for_tiles
    def _(t):
        @pl.when(owner_of(t) != c)
        def _():
            pick_copy(t).wait_send()

    for k in range(CHUNKS):
        for child, (cond, dev) in enumerate(pan_children(k)):
            @pl.when(cond)
            def _():
                pan_copy(k, child, dev).wait_send()

    @pl.when(c == 0)
    def _():
        for dst in range(1, COLS):
            top_copy(dst).wait_send()

    @pl.when(is_owner)
    def _():
        for k in range(1, Z):
            z_copy(k).wait_send()

    for q in range(RING):
        x_copy(first + q).wait_send()


def store_kernel(src, dst, sems):
    part = src.shape[0] // CHUNKS
    copies = [
        pltpu.make_async_copy(
            src.at[pl.ds(k * part, part)], dst.at[pl.ds(k * part, part)], sems.at[k]
        )
        for k in range(CHUNKS)
    ]
    for copy in copies:
        copy.start()
    for copy in copies:
        copy.wait()


def store(block):
    return pl.pallas_call(
        store_kernel,
        out_shape=jax.ShapeDtypeStruct(block.shape, block.dtype),
        in_specs=[pl.BlockSpec(memory_space=pltpu.VMEM)],
        out_specs=pl.BlockSpec(memory_space=pltpu.HBM),
        scratch_shapes=[pltpu.SemaphoreType.DMA((CHUNKS,))],
        compiler_params=pltpu.CompilerParams(vmem_limit_bytes=1 << 20),
        name="store",
    )(block)


def fast_update(matrix, inverse, pivots):
    rows, cols = matrix.shape
    tiles = cols // LANES
    dma = pltpu.SemaphoreType.DMA
    updated = pl.pallas_call(
        update_kernel,
        out_shape=pltpu.VMEM((rows, cols), jnp.float32),
        in_specs=[
            pl.BlockSpec(memory_space=pltpu.HBM),
            pl.BlockSpec(memory_space=pltpu.VMEM),
            pl.BlockSpec(memory_space=pltpu.VMEM),
        ],
        out_specs=pl.BlockSpec(memory_space=pltpu.VMEM),
        scratch_shapes=[
            pltpu.VMEM((tiles, CAP, LANES), jnp.float32),
            pltpu.VMEM((COLS, CAP, LANES), jnp.float32),
            pltpu.VMEM((CHUNKS, rows // CHUNKS, NB), jnp.bfloat16),
            pltpu.VMEM((tiles, NB, LANES), jnp.bfloat16),
            pltpu.VMEM((COLS, CAP, cols), jnp.bfloat16),
            pltpu.VMEM((LANES, cols), jnp.bfloat16),
            pltpu.VMEM((NB, COLS * CAP), jnp.float32),
            pltpu.VMEM((rows, LANES), jnp.bfloat16),
            pltpu.VMEM((1, LANES), jnp.int32),
            pltpu.SMEM((1, LANES), jnp.int32),
            dma((CHUNKS,)), dma, dma, dma((tiles,)), dma((COLS,)),
            dma((CHUNKS, 5)), dma((CHUNKS,)), dma((COLS,)), dma,
            dma((Z,)), dma((tiles,)), dma((tiles,)),
        ],
        compiler_params=pltpu.CompilerParams(
            collective_id=0, has_side_effects=True, vmem_limit_bytes=16 << 20
        ),
        name="update",
    )(matrix, inverse, pivots.reshape(1, NB))
    return store(updated)


def per_device(matrix, inverse, pivots):
    rows = matrix.shape[0]
    held = jnp.sum((pivots[:, None] // rows == jnp.arange(COLS)[None, :]).astype(jnp.int32), axis=0)
    fits = jnp.max(held) <= CAP
    return lax.cond(fits, fast_update, any_pivots, matrix, inverse, pivots)


def solution(mesh):
    return jax.shard_map(
        per_device,
        mesh=mesh,
        in_specs=(P("col", "row"), P(), P()),
        out_specs=P("col", "row"),
        check_vma=False,
    )
```

time: 491 us -> 70.2 us (0.14)
  waiting for transfers between devices: 413 us -> 0 us
  Pallas kernels: 0 us -> 49.1 us
  local copies, waits for them, and re-layouts: 40 us -> 5.95 us
  other arithmetic: 13.4 us -> 0.76 us
  matrix products: 7.98 us -> 0 us
    psum x3 -> x0, waiting for transfers between devices: 413 us -> none  [the longest x2 267 us: from_root(): return lax.psum(jnp.where(mine, array, jnp.zeros_like(array)), axis)]
    pallas_call x0 -> x2, Pallas kernels: none -> 49.1 us  [the longest x1 46.4 us: fast_update(): pl.pallas_call(update_kernel, out_shape=pltpu.VMEM((rows, cols), jnp.floa...]
    scatter x2 -> x0, local copies, waits for them, and re-layouts: 13.6 us -> none  [per_device(): swapped = matrix.at[target].set(top_block, mode='drop')]
    select_n x5 -> x1, other arithmetic: 9.73 us -> 0.01 us  [per_device(): pivots[:, None] // rows == jnp.arange(COLS)[None, :]]
    dot_general x2 -> x0, matrix products: 7.98 us -> none  [the longest x1 4.03 us: solve_rows(): jnp.dot(inverse, block, precision=lax.Precision.HIGHEST, preferred_elemen...]
    unnamed x6 -> x5, local copies, waits for them, and re-layouts: 12.6 us -> 5.95 us
    select_n x1 -> x0, local copies, waits for them, and re-layouts: 6.56 us -> none  [per_device(): return jnp.where((column_ids < block_width)[None, :], matrix, updated)]
    gather x1 -> x0, local copies, waits for them, and re-layouts: 5.87 us -> none  [per_device(): picked = jnp.take(matrix, jnp.clip(local_rows, 0, rows_dev - 1), axis=0)]
  transfers between devices with their start and end apart: 3 -> 0, of which waited for: 3 -> 0; matrix products, arithmetic and copies ran while one was open for 6% -> 0% of each run, Pallas kernels for 0% -> 0%
where the time goes in v1:
time: 70.2 us; the launch traced here: 70.1 us
  Pallas kernels  49.1 us (70%)
  between operations  14.1 us (20%)
  local copies, waits for them, and re-layouts  5.95 us (8%)
  other arithmetic  0.76 us (1%)
    pallas_call x1, Pallas kernels, fast_update(): pl.pallas_call(update_kernel, out_shape=pltpu.VMEM((rows, cols), jnp.floa...  46.4 us
    unnamed x5, local copies, waits for them, and re-layouts  5.95 us
    pallas_call x1, Pallas kernels, store(): pl.pallas_call(store_kernel, out_shape=jax.ShapeDtypeStruct(block.shape,...  2.73 us

profile of v1, /device:TPU:49, one launch (start us, length us, event | category | flops | bytes accessed | tf_op | source)
XLA Modules:
  0.0 70.1 jit_solution(3443798287977078612)
XLA Ops:
  6.5 0.0 copy-start
  6.5 0.0 copy-start.1
  6.5 5.9 %copy.38 = f32[1024,1536]{1,0:T(8,128)} copy(f32[1024,1536]{1,0:T(8,128)} %param.7) | data formatting | bytes 12582912
  12.5 0.0 copy-done.1
  12.5 0.1 convert_reduce_fusion
  12.6 0.6 reduce_max.9
  13.9 0.0 copy-done
  13.9 49.4 %conditional.1 = (f32[1024,1536]{1,0:T(8,128)}) conditional(s32[]{:T(128)} %convert_element_type.15, (s32[256]{0:T(256)S(1)}, f32[1024,1536]{1,0:T(8,128)}, f32[256,256]{1,0:T(8,128)S(1)}) %tuple.38, (s32[256]{0:T(256)S(1)}, f32[1024,1536]{1,0:T(8,128)}, f32[256,256]{1,0:T(8,128)S(1)}) %tuple.39), branch_computations={%region_2.7_spmd, %region_7.8_spmd} | conditional | flops 2021270272 | bytes 122174696 | solution.py:391
  13.9 46.4 %update.1.src = f32[1024,1536]{1,0:T(8,128)S(1)} custom-call(f32[1024,1536]{1,0:T(8,128)} %get-tuple-element.35.mat_hbm, f32[256,256]{1,0:T(8,128)S(1)} %get-tuple-element.36.inv_ref, s32[1,256]{1,0:T(1,128)S(1)} %bitcast.6), custom_call_target="tpu_custom_call" | custom-call | tf_op jit(solution)/shard_map/cond/branch_1_fun/update/pallas_call | solution.py:355
  60.3 2.7 %store.1 = f32[1024,1536]{1,0:T(8,128)} custom-call(f32[1024,1536]{1,0:T(8,128)S(1)} %update.1.src), custom_call_target="tpu_custom_call" | custom-call | tf_op jit(solution)/shard_map/cond/branch_1_fun/store/pallas_call | solution.py:340
  (1 shorter events, 0.0 us)
Async XLA Ops:
  6.5 7.4 %copy-start = (f32[256,256]{1,0:T(8,128)S(1)}, f32[256,256]{1,0:T(8,128)}, u32[]{:S(2)}) copy-start(f32[256,256]{1,0:T(8,128)} %param.8) | copy-start | bytes 786436
  6.5 5.9 %copy-start.1 = (s32[256]{0:T(256)S(1)}, s32[256]{0:T(256)}, u32[]{:S(2)}) copy-start(s32[256]{0:T(256)} %param.9) | copy-start | bytes 3076

commit v2 on v1

--- a/solution.py
+++ b/solution.py
@@ -17,9 +17,15 @@
 RING = 6
 
 
+def total(array, axis):
+    for step in (1, 2, 4, 8):
+        array = array + lax.ppermute(array, axis, [(i, i ^ step) for i in range(COLS)])
+    return array
+
+
 def from_root(array, axis, root):
     mine = lax.axis_index(axis) == root
-    return lax.psum(jnp.where(mine, array, jnp.zeros_like(array)), axis)
+    return total(jnp.where(mine, array, jnp.zeros_like(array)), axis)
 
 
 def any_pivots(matrix, inverse, pivots):
@@ -32,20 +38,22 @@
     picked = jnp.take(matrix, jnp.clip(local_rows, 0, rows_dev - 1), axis=0)
     picked = jnp.where(owned_here[:, None], picked, 0.0)
     panel_rows = from_root(matrix[:, :block_width].astype(jnp.bfloat16), "row", 0)
-    pivot_block = lax.psum(picked, "col")
+    pivot_block = total(picked, "col")
     top_block = from_root(matrix[:block_width].astype(jnp.bfloat16), "col", 0).astype(jnp.float32)
     upper_rows = jnp.dot(
         inverse, pivot_block, precision=lax.Precision.HIGHEST, preferred_element_type=jnp.float32
     )
-    target = jnp.where(owned_here, local_rows, rows_dev)
-    swapped = matrix.at[target].set(top_block, mode="drop")
+    row_ids = jnp.arange(rows_dev)
+    hit = row_ids[:, None] == local_rows[None, :]
+    source = jnp.sum(jnp.where(hit, jnp.arange(block_width)[None, :], 0), axis=1)
+    moved = jnp.take(top_block, source, axis=0)
+    swapped = jnp.where(jnp.any(hit, axis=1)[:, None], moved, matrix)
     product = jnp.dot(
         panel_rows, upper_rows.astype(jnp.bfloat16), preferred_element_type=jnp.float32
     )
     updated = swapped - product
-    updated = updated.at[:block_width].set(
-        jnp.where(grid_col == 0, upper_rows, updated[:block_width])
-    )
+    solved = jnp.concatenate([upper_rows, jnp.zeros_like(updated[block_width:])], axis=0)
+    updated = jnp.where(((grid_col == 0) & (row_ids < block_width))[:, None], solved, updated)
     column_ids = grid_row * cols_dev + jnp.arange(cols_dev)
     return jnp.where((column_ids < block_width)[None, :], matrix, updated)
 

time: 70.2 us -> 52.7 us (0.75)
  between operations: 14.1 us -> 0.84 us
  local copies, waits for them, and re-layouts: 5.95 us -> 0 us
  Pallas kernels: 49.1 us -> 50 us
    unnamed x5 -> x0, local copies, waits for them, and re-layouts: 5.95 us -> none
    pallas_call x1, Pallas kernels: 46.4 us -> 47.3 us  [fast_update(): pl.pallas_call(update_kernel, out_shape=pltpu.VMEM((rows, cols), jnp.floa...]
where the time goes in v2:
time: 52.7 us; the launch traced here: 52.6 us
  Pallas kernels  50 us (95%)
  other arithmetic  1.44 us (3%)
  between operations  0.84 us (2%)
    pallas_call x1, Pallas kernels, fast_update(): pl.pallas_call(update_kernel, out_shape=pltpu.VMEM((rows, cols), jnp.floa...  47.3 us
    pallas_call x1, Pallas kernels, store(): pl.pallas_call(store_kernel, out_shape=jax.ShapeDtypeStruct(block.shape,...  2.73 us

profile of v2, /device:TPU:49, one launch (start us, length us, event | category | flops | bytes accessed | tf_op | source)
XLA Modules:
  0.0 52.6 jit_solution(11886492305482081030)
XLA Ops:
  0.0 0.7 %and_select_fusion = s32[256]{0:T(256)S(1)} fusion(s32[256]{0:T(256)} %param.7), kind=kLoop, calls=%fused_computation.28 | loop fusion | flops 3840 | bytes 2048 | tf_op jit(solution)/shard_map/jit(floor_divide)/jit(_where)/select_n | solution.py:397
  0.7 0.1 convert_reduce_fusion
  0.8 0.6 %reduce_max.9 = s32[]{:T(128)} reduce(s32[16]{0:T(128)S(1)} %convert_reduce_fusion, s32[]{:T(128)} %constant.73.clone.1), dimensions={0}, to_apply=%region_1.2 | reduce | flops 15 | bytes 72 | tf_op jit(solution)/shard_map/reduce_max | solution.py:398
  2.1 50.3 %conditional.1 = (f32[1024,1536]{1,0:T(8,128)}) conditional(s32[]{:T(128)} %convert_element_type.15, (s32[256]{0:T(256)}, f32[1024,1536]{1,0:T(8,128)}, f32[256,256]{1,0:T(8,128)}) %tuple.11, (s32[256]{0:T(256)}, f32[1024,1536]{1,0:T(8,128)}, f32[256,256]{1,0:T(8,128)}) %tuple.11), branch_computations={%region_2.5_spmd, %region_5.6_spmd} | conditional | flops 2031896320 | bytes 202952864 | solution.py:399
  2.3 47.3 %update.1.src = f32[1024,1536]{1,0:T(8,128)S(1)} custom-call(f32[1024,1536]{1,0:T(8,128)} %get-tuple-element.23.mat_hbm, f32[256,256]{1,0:T(8,128)} %get-tuple-element.24.inv_ref, s32[1,256]{1,0:T(1,128)} %bitcast.8), custom_call_target="tpu_custom_call" | custom-call | tf_op jit(solution)/shard_map/cond/branch_1_fun/update/pallas_call | solution.py:363
  49.6 2.7 %store.1 = f32[1024,1536]{1,0:T(8,128)} custom-call(f32[1024,1536]{1,0:T(8,128)S(1)} %update.1.src), custom_call_target="tpu_custom_call" | custom-call | tf_op jit(solution)/shard_map/cond/branch_1_fun/store/pallas_call | solution.py:348

commit v3 on v2

--- a/solution.py
+++ b/solution.py
@@ -15,6 +15,9 @@
 COLS = 16
 CHUNKS = 4
 RING = 6
+DIRECT = (2, 6, 1, 7)
+RELAYED = (11, 10, 9)
+TOP_ORDER = (12, 4, 11, 3, 14, 13, 5, 10, 2, 15, 6, 9, 1, 7, 8)
 
 
 def total(array, axis):
@@ -59,10 +62,10 @@
 
 
 def update_kernel(
-    mat_hbm, inv_ref, piv_ref, out_ref,
+    mat_hbm, inv_ref, piv_ref, out_ref, most_ref,
     picked, gathered, panel, upper, tops, top, perm, hits, idx_v, idx_s,
     load_sem, idx_sem, own_sem, sp_send, sp_recv, pan_send, pan_recv, top_send, top_recv,
-    z_send, x_send, up_recv,
+    z_send, f_send, x_send, up_recv, half_recv, hand, hand_send, hand_recv, mask,
 ):
     rows, cols = out_ref.shape
     tiles = cols // LANES
@@ -80,29 +83,32 @@
 
     def owner_of(t):
         q = t % RING
-        return (t // RING) * Z + (q + 1 + (q >= 3).astype(jnp.int32) + 2 * core) % Z
-
-    zq = (z - 2 * core + Z) % Z
-    is_owner = (zq != 0) & (zq != 4)
-    my_tile = xhi * RING + jnp.maximum(zq - 1 - (zq > 4).astype(jnp.int32), 0)
+        return (t // RING) * Z + q + 1 + (q >= 3).astype(jnp.int32)
+
+    def tile_of(away):
+        zq = (z + away + Z) % Z
+        return xhi * RING + jnp.maximum(zq - 1 - (zq > 4).astype(jnp.int32), 0), zq % 4 != 0
+
+    my_tile, is_owner = tile_of(0)
+
+    loads = [
+        pltpu.make_async_copy(
+            mat_hbm.at[pl.ds(k * part, part)], out_ref.at[pl.ds(k * part, part)], load_sem.at[k]
+        )
+        for k in range(CHUNKS)
+    ]
+    for load in loads:
+        load.start()
 
     barrier = pltpu.get_barrier_semaphore()
     for k in range(1, COLS):
         pl.semaphore_signal(barrier, inc=1, device_id=col_dev((c + k) % COLS), device_id_type=MESH)
     for dev in (
         row_dev(xlo, y, 1 - core), row_dev(xlo, (y + 1) % 4, core),
-        row_dev(xlo, (y + 3) % 4, core), row_dev(1 - xlo, y, core),
+        row_dev(xlo, (y + 2) % 4, core), row_dev(xlo, (y + 3) % 4, core), row_dev(1 - xlo, y, core),
+        row_dev(xlo, (y + 1) % 4, 1 - core), row_dev(xlo, (y + 3) % 4, 1 - core), row_dev(1 - xlo, y, 1 - core),
     ):
         pl.semaphore_signal(barrier, inc=1, device_id=dev, device_id_type=MESH)
-
-    loads = [
-        pltpu.make_async_copy(
-            mat_hbm.at[pl.ds(k * part, part)], out_ref.at[pl.ds(k * part, part)], load_sem.at[k]
-        )
-        for k in range(CHUNKS)
-    ]
-    for load in loads:
-        load.start()
 
     i_id = lax.broadcasted_iota(jnp.int32, (NB, NB), 0)
     j_id = lax.broadcasted_iota(jnp.int32, (NB, NB), 1)
@@ -110,7 +116,9 @@
     piv_col = piv_row.T
     own_row, own_col = piv_row // rows, piv_col // rows
     rank = jnp.sum(((own_row == own_col) & (i_id < j_id)).astype(jnp.int32), axis=0, keepdims=True)
-    slot_row = jnp.broadcast_to(own_row[:1] * CAP + rank, (NB, NB))
+    most_ref[0, 0] = jnp.max(rank)
+    slot = jnp.where(rank < CAP, own_row[:1] * CAP + rank, -1)
+    slot_row = jnp.broadcast_to(slot, (NB, NB))
     slot_col = slot_row.T
     lane = j_id[:, :LANES]
     match = (slot_col[:, :LANES] == c * CAP + lane) & (lane < CAP)
@@ -132,59 +140,6 @@
         for t in range(tiles):
             picked[t, k : k + 1, :] = row[:, t * LANES : (t + 1) * LANES]
 
-    pl.semaphore_wait(barrier, COLS - 1 + 4)
-
-    def pick_copy(t):
-        return pltpu.make_async_remote_copy(
-            src_ref=picked.at[t], dst_ref=gathered.at[c], send_sem=sp_send.at[t],
-            recv_sem=sp_recv.at[c], device_id=col_dev(owner_of(t)), device_id_type=MESH,
-        )
-
-    def for_tiles(body):
-        lax.fori_loop(0, tiles, lambda t, _: (body(t), 0)[1], 0)
-
-    @for_tiles
-    def _(t):
-        @pl.when(owner_of(t) != c)
-        def _():
-            pick_copy(t).start()
-
-    def pan_copy(k, child, dev):
-        return pltpu.make_async_remote_copy(
-            src_ref=panel.at[k], dst_ref=panel.at[k], send_sem=pan_send.at[k, child],
-            recv_sem=pan_recv.at[k], device_id=dev, device_id_type=MESH,
-        )
-
-    def pan_children(k):
-        return [
-            ((core == 0) & (y == 0), row_dev(xlo, 1, 0)),
-            ((core == 0) & (y == 0), row_dev(xlo, 3, 0)),
-            ((core == 0) & (y == 0) & (xlo == 0), row_dev(1, 0, 0)),
-            ((core == 0) & (y == (1 if k < CHUNKS // 2 else 3)), row_dev(xlo, 2, 0)),
-            (core == 0, row_dev(xlo, y, 1)),
-        ]
-
-    def pan_forward(k):
-        for child, (cond, dev) in enumerate(pan_children(k)):
-            @pl.when(cond)
-            def _():
-                pan_copy(k, child, dev).start()
-
-    def pan_wait(k):
-        pan_copy(k, 0, row_dev(xlo, y, 1 - core)).wait_recv()
-
-    @pl.when(r == 0)
-    def _():
-        for k in range(CHUNKS):
-            panel[k] = out_ref[k * part : (k + 1) * part, :NB].astype(jnp.bfloat16)
-            pan_forward(k)
-
-    def top_copy(dst):
-        return pltpu.make_async_remote_copy(
-            src_ref=tops.at[dst], dst_ref=top.at[pl.ds(0, CAP)], send_sem=top_send.at[dst],
-            recv_sem=top_recv, device_id=col_dev(dst), device_id_type=MESH,
-        )
-
     @pl.when(c == 0)
     def _():
         s_id = lax.broadcasted_iota(jnp.int32, (NB, NB), 0)
@@ -194,9 +149,95 @@
             pick = (slot_row == s_id + h * NB).astype(jnp.float32).astype(jnp.bfloat16)
             sent = jnp.dot(pick, block, preferred_element_type=jnp.float32).astype(jnp.bfloat16)
             tops[h * half : (h + 1) * half] = sent.reshape(half, CAP, cols)
-            for dst in range(max(1, h * half), (h + 1) * half):
+
+    @pl.when(r == 0)
+    def _():
+        for k in range(CHUNKS):
+            panel[k] = out_ref[k * part : (k + 1) * part, :NB].astype(jnp.bfloat16)
+
+    pl.semaphore_wait(barrier, COLS - 1 + 8)
+
+    def pick_copy(t):
+        return pltpu.make_async_remote_copy(
+            src_ref=picked.at[t], dst_ref=gathered.at[c], send_sem=sp_send.at[t],
+            recv_sem=sp_recv.at[c], device_id=col_dev(owner_of(t)), device_id_type=MESH,
+        )
+
+    def for_tiles(body):
+        lax.fori_loop(0, tiles, lambda t, _: (body(t), 0)[1], 0)
+
+    @for_tiles
+    def _(t):
+        @pl.when(owner_of(t) != c)
+        def _():
+            pick_copy(t).start()
+
+    def pan_copy(k, child, dev):
+        return pltpu.make_async_remote_copy(
+            src_ref=panel.at[k], dst_ref=panel.at[k], send_sem=pan_send.at[k, child],
+            recv_sem=pan_recv.at[k], device_id=dev, device_id_type=MESH,
+        )
+
+    def pan_children(k):
+        return [
+            (r == 0, row_dev(0, 1, 0)),
+            (r == 1, row_dev(0, 3, 0)),
+            (r == 1, row_dev(1, 0, 0)),
+            ((core == 0) & (xlo == 0) & ((y == 1) | (y == 3)), row_dev(1, y, 0)),
+            ((core == 0) & (xlo == 0) & (y == (1 if k < CHUNKS // 2 else 3)), row_dev(0, 2, 0)),
+            ((core == 0) & (xlo == 1) & (y == 0), row_dev(1, 2, 0)),
+            (core == 0, row_dev(xlo, y, 1)),
+        ]
+
+    def pan_forward(k):
+        for child, (cond, dev) in enumerate(pan_children(k)):
+            @pl.when(cond)
+            def _():
+                pan_copy(k, child, dev).start()
+
+    def pan_wait(k):
+        pan_copy(k, 0, row_dev(xlo, y, 1 - core)).wait_recv()
+
+    def top_copy(dst):
+        by_hand = dst in RELAYED
+        slot_ = RELAYED.index(dst) if by_hand else 0
+        return pltpu.make_async_remote_copy(
+            src_ref=tops.at[dst], dst_ref=hand.at[slot_] if by_hand else top.at[pl.ds(0, CAP)],
+            send_sem=top_send.at[dst], recv_sem=hand_recv.at[slot_] if by_hand else top_recv,
+            device_id=col_dev(Z if by_hand else dst), device_id_type=MESH,
+        )
+
+    def hand_copy(dst):
+        slot_ = RELAYED.index(dst)
+        return pltpu.make_async_remote_copy(
+            src_ref=hand.at[slot_], dst_ref=top.at[pl.ds(0, CAP)], send_sem=hand_send.at[slot_],
+            recv_sem=top_recv, device_id=col_dev(dst), device_id_type=MESH,
+        )
+
+    @pl.when(r == 0)
+    def _():
+        for k in range(CHUNKS):
+            pan_forward(k)
+
+    for k in range(CHUNKS):
+        @pl.when(c == 0)
+        def _():
+            for dst in TOP_ORDER[4 * k : 4 * k + 4]:
                 top_copy(dst).start()
+
+    @pl.when(c == 0)
+    def _():
         pltpu.make_async_copy(tops.at[0], top.at[pl.ds(0, CAP)], own_sem).start()
+
+    @pl.when(r == 1)
+    def _():
+        for k in range(CHUNKS):
+            pan_wait(k)
+            pan_forward(k)
+
+    mask[...] = jnp.dot(
+        hits[...], jnp.ones((LANES, LANES), jnp.bfloat16), preferred_element_type=jnp.float32
+    )
 
     for h in range(COLS * CAP // NB):
         place = (slot_col == j_id + h * NB).astype(jnp.float32)
@@ -206,15 +247,9 @@
 
     depth_one = (core == 0) & (((xlo == 0) & ((y == 1) | (y == 3))) | ((xlo == 1) & (y == 0)))
 
-    @pl.when(depth_one)
-    def _():
-        for k in range(CHUNKS):
-            pan_wait(k)
-            pan_forward(k)
-
     def z_copy(k):
         return pltpu.make_async_remote_copy(
-            src_ref=upper.at[my_tile], dst_ref=upper.at[my_tile], send_sem=z_send.at[k],
+            src_ref=upper.at[my_tile], dst_ref=upper.at[my_tile], send_sem=z_send.at[DIRECT.index(k)],
             recv_sem=up_recv.at[my_tile], device_id=col_dev(xhi * Z + (z + k) % Z), device_id_type=MESH,
         )
 
@@ -238,71 +273,123 @@
             precision=lax.Precision.HIGHEST, preferred_element_type=jnp.float32,
         )
         upper[my_tile] = solved.astype(jnp.bfloat16)
-        for k in (4, 3, 5, 2, 6, 1, 7):
+        for k in DIRECT:
             z_copy(k).start()
         x_copy(my_tile).start()
 
-    @pl.when(jnp.logical_not(depth_one) & (r != 0))
+    def forward_copy(t, sign, to_four):
+        half = NB // 2
+        which = (1 - sign) // 2
+        part_ref = upper.at[t, pl.ds(which * half, half)] if to_four else upper.at[t]
+        return pltpu.make_async_remote_copy(
+            src_ref=part_ref, dst_ref=part_ref, send_sem=f_send.at[which, int(to_four)],
+            recv_sem=half_recv.at[which, t] if to_four else up_recv.at[t],
+            device_id=col_dev(xhi * Z + (z + (2 if to_four else 1) * sign + Z) % Z), device_id_type=MESH,
+        )
+
+    def ring(away):
+        t, owned = tile_of(away)
+
+        @pl.when(owned)
+        def _():
+            if away == 4:
+                forward_copy(t, 1, True).wait_recv()
+                forward_copy(t, -1, True).wait_recv()
+            else:
+                x_copy(t).wait_recv()
+            if abs(away) == 2:
+                forward_copy(t, -away // 2, False).start()
+                forward_copy(t, -away // 2, True).start()
+            x_copy(t).start()
+
+    for k in range(max(CHUNKS, len(RELAYED))):
+        if k < CHUNKS:
+            @pl.when(depth_one)
+            def _():
+                pan_wait(k)
+                pan_forward(k)
+
+        @pl.when(c == Z)
+        def _():
+            for dst in RELAYED[k : k + 1]:
+                top_copy(dst).wait_recv()
+                hand_copy(dst).start()
+
+    ring(-2)
+    ring(2)
+
+    for away in (-1, 1, -3, 3, 4):
+        ring(away)
+
+    @pl.when(jnp.logical_not(depth_one) & (r > 1))
     def _():
         for k in range(CHUNKS):
             pan_wait(k)
             pan_forward(k)
 
+    @pl.when(c == 0)
+    def _():
+        pltpu.make_async_copy(tops.at[0], top.at[pl.ds(0, CAP)], own_sem).wait()
+
+    @pl.when(c != 0)
+    def _():
+        top_copy(1).wait_recv()
+
     first = xhi * RING
-    for q in range(RING):
-        @pl.when((first + q != my_tile) | jnp.logical_not(is_owner))
-        def _():
-            x_copy(first + q).wait_recv()
-            x_copy(first + q).start()
-
-    @pl.when(c == 0)
-    def _():
-        pltpu.make_async_copy(tops.at[0], top.at[pl.ds(0, CAP)], own_sem).wait()
-
-    @pl.when(c != 0)
-    def _():
-        top_copy(c).wait_recv()
-
-    def trailing(t):
-        return (r != 0) | (t >= NB // LANES)
-
-    def columns(t):
-        return pl.ds(pl.multiple_of(t * LANES, LANES), LANES)
-
-    taken = jnp.sum(hits[...].astype(jnp.float32), axis=1, keepdims=True) > 0.5
-
-    @for_tiles
-    def _(t):
-        @pl.when(trailing(t))
-        def _():
-            moved = jnp.dot(hits[...], top[:, columns(t)], preferred_element_type=jnp.float32)
-            out_ref[:, columns(t)] = jnp.where(taken, moved, out_ref[:, columns(t)])
-
-    def apply(t):
-        @pl.when(trailing(t))
-        def _():
-            for k in range(CHUNKS):
-                rows_k = pl.ds(k * part, part)
-                out_ref[rows_k, columns(t)] = out_ref[rows_k, columns(t)] - jnp.dot(
-                    panel[k], upper[t], preferred_element_type=jnp.float32
-                )
-
-            @pl.when(c == 0)
+
+    def each_pair(base, body):
+        def step(p, _):
+            pair = base // 2 + p
+
+            @pl.when((r != 0) | (pair > 0))
             def _():
-                out_ref[:NB, columns(t)] = upper[t].astype(jnp.float32)
-
-    def loop(body):
-        lax.fori_loop(0, RING, lambda q, _: (body(q), 0)[1], 0)
-
-    @loop
-    def _(q):
-        apply(first + q)
-
-    @loop
-    def _(q):
-        t = (1 - xhi) * RING + q
-        x_copy(t).wait_recv()
-        apply(t)
+                body(pair, pl.ds(pl.multiple_of(pair * 2 * LANES, 2 * LANES), 2 * LANES))
+
+            return 0
+
+        lax.fori_loop(0, RING // 2, step, 0)
+
+    def swapped(k, cols_p):
+        rows_k = pl.ds(k * part, part)
+        moved = jnp.dot(hits[rows_k, :], top[:, cols_p], preferred_element_type=jnp.float32)
+        taken = jnp.concatenate([mask[rows_k, :]] * 2, axis=1) > 0.5
+        return jnp.where(taken, moved, out_ref[rows_k, cols_p])
+
+    def product(k, solved):
+        return jnp.dot(panel[k], solved, preferred_element_type=jnp.float32)
+
+    def finish(solved, cols_p):
+        @pl.when(c == 0)
+        def _():
+            out_ref[:NB, cols_p] = solved.astype(jnp.float32)
+
+    def own_pair(pair, cols_p):
+        solved = jnp.concatenate([upper[2 * pair], upper[2 * pair + 1]], axis=1)
+        for k in range(CHUNKS):
+            out_ref[pl.ds(k * part, part), cols_p] = swapped(k, cols_p) - product(k, solved)
+        finish(solved, cols_p)
+
+    def base_pair(pair, cols_p):
+        for k in range(CHUNKS):
+            out_ref[pl.ds(k * part, part), cols_p] = swapped(k, cols_p)
+
+    def partner_pair(pair, cols_p):
+        solved = jnp.concatenate([upper[2 * pair], upper[2 * pair + 1]], axis=1)
+        for k in range(CHUNKS):
+            rows_k = pl.ds(k * part, part)
+            out_ref[rows_k, cols_p] = out_ref[rows_k, cols_p] - product(k, solved)
+        finish(solved, cols_p)
+
+    each_pair(first, own_pair)
+    each_pair(RING - first, base_pair)
+    for q in range(RING // 2):
+        pair = (RING - first) // 2 + q
+        x_copy(2 * pair).wait_recv()
+        x_copy(2 * pair + 1).wait_recv()
+
+        @pl.when((r != 0) | (pair > 0))
+        def _():
+            partner_pair(pair, pl.ds(pl.multiple_of(pair * 2 * LANES, 2 * LANES), 2 * LANES))
 
     @for_tiles
     def _(t):
@@ -323,8 +410,21 @@
 
     @pl.when(is_owner)
     def _():
-        for k in range(1, Z):
+        for k in DIRECT:
             z_copy(k).wait_send()
+
+    for away in (-2, 2):
+        t, owned = tile_of(away)
+
+        @pl.when(owned)
+        def _():
+            forward_copy(t, -away // 2, False).wait_send()
+            forward_copy(t, -away // 2, True).wait_send()
+
+    @pl.when(c == Z)
+    def _():
+        for dst in RELAYED:
+            hand_copy(dst).wait_send()
 
     for q in range(RING):
         x_copy(first + q).wait_send()
@@ -360,15 +460,15 @@
     rows, cols = matrix.shape
     tiles = cols // LANES
     dma = pltpu.SemaphoreType.DMA
-    updated = pl.pallas_call(
+    return pl.pallas_call(
         update_kernel,
-        out_shape=pltpu.VMEM((rows, cols), jnp.float32),
+        out_shape=(pltpu.VMEM((rows, cols), jnp.float32), jax.ShapeDtypeStruct((1, 1), jnp.int32)),
         in_specs=[
             pl.BlockSpec(memory_space=pltpu.HBM),
             pl.BlockSpec(memory_space=pltpu.VMEM),
             pl.BlockSpec(memory_space=pltpu.VMEM),
         ],
-        out_specs=pl.BlockSpec(memory_space=pltpu.VMEM),
+        out_specs=(pl.BlockSpec(memory_space=pltpu.VMEM), pl.BlockSpec(memory_space=pltpu.SMEM)),
         scratch_shapes=[
             pltpu.VMEM((tiles, CAP, LANES), jnp.float32),
             pltpu.VMEM((COLS, CAP, LANES), jnp.float32),
@@ -381,22 +481,26 @@
             pltpu.VMEM((1, LANES), jnp.int32),
             pltpu.SMEM((1, LANES), jnp.int32),
             dma((CHUNKS,)), dma, dma, dma((tiles,)), dma((COLS,)),
-            dma((CHUNKS, 5)), dma((CHUNKS,)), dma((COLS,)), dma,
-            dma((Z,)), dma((tiles,)), dma((tiles,)),
+            dma((CHUNKS, 7)), dma((CHUNKS,)), dma((COLS,)), dma,
+            dma((len(DIRECT),)), dma((2, 2)), dma((tiles,)), dma((tiles,)), dma((2, tiles)),
+            pltpu.VMEM((len(RELAYED), CAP, cols), jnp.bfloat16), dma((len(RELAYED),)), dma((len(RELAYED),)),
+            pltpu.VMEM((rows, LANES), jnp.float32),
         ],
         compiler_params=pltpu.CompilerParams(
             collective_id=0, has_side_effects=True, vmem_limit_bytes=16 << 20
         ),
         name="update",
     )(matrix, inverse, pivots.reshape(1, NB))
-    return store(updated)
 
 
 def per_device(matrix, inverse, pivots):
-    rows = matrix.shape[0]
-    held = jnp.sum((pivots[:, None] // rows == jnp.arange(COLS)[None, :]).astype(jnp.int32), axis=0)
-    fits = jnp.max(held) <= CAP
-    return lax.cond(fits, fast_update, any_pivots, matrix, inverse, pivots)
+    updated, most = fast_update(matrix, inverse, pivots)
+    return lax.cond(
+        most[0, 0] < CAP,
+        lambda block, *_: block,
+        lambda _, *args: any_pivots(*args),
+        store(updated), matrix, inverse, pivots,
+    )
 
 
 def solution(mesh):

time: 52.7 us -> 43.4 us (0.82)
  Pallas kernels: 50 us -> 42.2 us
  other arithmetic: 1.44 us -> 0 us
    pallas_call x1, Pallas kernels: 47.3 us -> 39.5 us  [fast_update(): pl.pallas_call(update_kernel, out_shape=(pltpu.VMEM((rows, cols), jnp.flo...]
    select_n x1 -> x0, other arithmetic: 0.69 us -> none  [per_device(): pivots[:, None] // rows == jnp.arange(COLS)[None, :]]
    reduce_max x1 -> x0, other arithmetic: 0.64 us -> none  [per_device(): fits = jnp.max(held) <= CAP]
where the time goes in v3:
time: 43.4 us; the launch traced here: 43.3 us
  Pallas kernels  42.2 us (97%)
  between operations  0.84 us (2%)
    pallas_call x1, Pallas kernels, fast_update(): pl.pallas_call(update_kernel, out_shape=(pltpu.VMEM((rows, cols), jnp.flo...  39.5 us
    pallas_call x1, Pallas kernels, store(): pl.pallas_call(store_kernel, out_shape=jax.ShapeDtypeStruct(block.shape,...  2.73 us

profile of v3, /device:TPU:49, one launch (start us, length us, event | category | flops | bytes accessed | tf_op | source)
XLA Modules:
  0.0 43.3 jit_solution(9290953762239088738)
XLA Ops:
  0.0 0.0 copy-start.3
  0.0 0.0 copy-start.4
  0.0 39.5 %update.1 = (f32[1024,1536]{1,0:T(8,128)S(1)}, s32[1,1]{1,0:T(1,128)}) custom-call(f32[1024,1536]{1,0:T(8,128)} %mat_hbm.1, f32[256,256]{1,0:T(8,128)} %inv_ref.1, s32[1,256]{1,0:T(1,128)} %bitcast.9), custom_call_target="tpu_custom_call" | custom-call | tf_op jit(solution)/shard_map/update/pallas_call | solution.py:463
  40.1 0.0 copy-done.3
  40.1 0.0 copy-done.4
  40.1 2.7 %store.1 = f32[1024,1536]{1,0:T(8,128)} custom-call(f32[1024,1536]{1,0:T(8,128)S(1)} %get-tuple-element.21.src), custom_call_target="tpu_custom_call" | custom-call | tf_op jit(solution)/shard_map/store/pallas_call | solution.py:448
  42.9 0.2 conditional.1
Async XLA Ops:
  0.0 40.1 %copy-start.3 = (f32[256,256]{1,0:T(8,128)S(1)}, f32[256,256]{1,0:T(8,128)}, u32[]{:S(2)}) copy-start(f32[256,256]{1,0:T(8,128)} %inv_ref.1) | copy-start | bytes 786436
  0.0 40.1 %copy-start.4 = (s32[256]{0:T(256)S(1)}, s32[256]{0:T(256)}, u32[]{:S(2)}) copy-start(s32[256]{0:T(256)} %param.7) | copy-start | bytes 3076

commit v4 on v3

--- a/solution.py
+++ b/solution.py
@@ -15,8 +15,8 @@
 COLS = 16
 CHUNKS = 4
 RING = 6
-DIRECT = (2, 6, 1, 7)
-RELAYED = (11, 10, 9)
+DIRECT = (1, 7, 2, 6)
+RELAYED = (12, 11, 10)
 TOP_ORDER = (12, 4, 11, 3, 14, 13, 5, 10, 2, 15, 6, 9, 1, 7, 8)
 
 

time: 43.4 us -> 42.7 us (0.984); the launches traced: 43.3 us -> 42.1 us
  Pallas kernels: 42.2 us -> 41 us
    pallas_call x1, Pallas kernels: 39.5 us -> 38.3 us  [fast_update(): pl.pallas_call(update_kernel, out_shape=(pltpu.VMEM((rows, cols), jnp.flo...]
where the time goes in v4:
time: 42.7 us; the launch traced here: 42.1 us
  Pallas kernels  41 us (96%)
  between operations  0.84 us (2%)
    pallas_call x1, Pallas kernels, fast_update(): pl.pallas_call(update_kernel, out_shape=(pltpu.VMEM((rows, cols), jnp.flo...  38.3 us
    pallas_call x1, Pallas kernels, store(): pl.pallas_call(store_kernel, out_shape=jax.ShapeDtypeStruct(block.shape,...  2.73 us

profile of v4, /device:TPU:49, one launch (start us, length us, event | category | flops | bytes accessed | tf_op | source)
XLA Modules:
  0.0 42.1 jit_solution(9742278261099813726)
XLA Ops:
  0.0 0.0 copy-start.3
  0.0 0.0 copy-start.4
  0.0 38.3 %update.1 = (f32[1024,1536]{1,0:T(8,128)S(1)}, s32[1,1]{1,0:T(1,128)}) custom-call(f32[1024,1536]{1,0:T(8,128)} %mat_hbm.1, f32[256,256]{1,0:T(8,128)} %inv_ref.1, s32[1,256]{1,0:T(1,128)} %bitcast.9), custom_call_target="tpu_custom_call" | custom-call | tf_op jit(solution)/shard_map/update/pallas_call | solution.py:463
  38.9 0.0 copy-done.3
  39.0 0.0 copy-done.4
  39.0 2.7 %store.1 = f32[1024,1536]{1,0:T(8,128)} custom-call(f32[1024,1536]{1,0:T(8,128)S(1)} %get-tuple-element.21.src), custom_call_target="tpu_custom_call" | custom-call | tf_op jit(solution)/shard_map/store/pallas_call | solution.py:448
  41.7 0.2 conditional.1
Async XLA Ops:
  0.0 39.0 %copy-start.3 = (f32[256,256]{1,0:T(8,128)S(1)}, f32[256,256]{1,0:T(8,128)}, u32[]{:S(2)}) copy-start(f32[256,256]{1,0:T(8,128)} %inv_ref.1) | copy-start | bytes 786436
  0.0 39.0 %copy-start.4 = (s32[256]{0:T(256)S(1)}, s32[256]{0:T(256)}, u32[]{:S(2)}) copy-start(s32[256]{0:T(256)} %param.7) | copy-start | bytes 3076
